TPU v7x, 256 devices: a whole 4x4x8 slice. The times are simulated.
256 devices in a mesh: shard: 16 (over x, z_hi, core), tp: 16 (over z_lo, y).
Axes of the slice: x: 4, y: 4, z: 8 (z_hi: 2, z_lo: 4; z = z_hi * 4 + z_lo), core: 2. Of those that a mesh axis runs over, the one named last changes fastest.
Arguments:
- master: float32 [8192, 4096], P('tp', 'shard'), may hold values from -0.56 to 0.56
- first_moment: float32 [8192, 4096], P('tp', 'shard'), may hold values from -0.5 to 0.5
- second_moment: float32 [8192, 4096], P('tp', 'shard'), may hold values from 0.01 to 0.2
- gradient: bfloat16 [8192, 4096], P('tp', 'shard'), may hold values from -4 to 4
- step_count: int32 [1], replicated, may hold values from 1 to 8
Outputs:
- new_master: float32 [8192, 4096], P('tp', 'shard')
- new_first: float32 [8192, 4096], P('tp', 'shard')
- new_second: float32 [8192, 4096], P('tp', 'shard')
- row_copy: bfloat16 [8192, 4096], P('tp')
- row_scales: bfloat16 [8192, 128], P('tp')
- col_copy: bfloat16 [16, 256, 8192], P(None, 'tp')
- col_scales: bfloat16 [16, 256, 256], P(None, 'tp')
All inputs are finite; a program needn't handle non-finite values.
Results may differ from a plain program's by a relative error of at most 0.011.
Values may be sent and summed in bfloat16 or wider, within the bound.
A program may use at most 64 MiB of HBM per device.

v0:
```python
import jax
import jax.numpy as jnp
from jax import lax
from jax.sharding import PartitionSpec as P

beta_one = 0.9
beta_two = 0.95
learn_rate = 0.02
epsilon = 1e-08
floor_value = 0.008
scale_unit = 64.0
block_size = 32


def quantize_blocks(values):
    dims = values.shape
    blocks = values.reshape(dims[:-1] + (dims[-1] // block_size, block_size))
    largest = jnp.max(jnp.abs(blocks), axis=-1)
    scales = (scale_unit * jnp.maximum(largest, floor_value)).astype(jnp.bfloat16)
    payload = (
        (scale_unit * blocks / scales.astype(jnp.float32)[..., None])
        .reshape(dims)
        .astype(jnp.bfloat16)
    )
    return (payload, scales)


def body(master, first_moment, second_moment, gradient, step_count):
    steps_done = step_count[0].astype(jnp.float32)
    grad_full = gradient.astype(jnp.float32)
    new_first = beta_one * first_moment + (1.0 - beta_one) * grad_full
    new_second = beta_two * second_moment + (1.0 - beta_two) * grad_full * grad_full
    corr_one = 1.0 - jnp.power(beta_one, steps_done)
    corr_two = 1.0 - jnp.power(beta_two, steps_done)
    update = new_first / corr_one / (jnp.sqrt(new_second / corr_two) + epsilon)
    new_master = master - learn_rate * update
    row_payload, row_scale = quantize_blocks(new_master)
    row_copy, row_scales = (
        lax.all_gather(row_payload, "shard", axis=1, tiled=True),
        lax.all_gather(row_scale, "shard", axis=1, tiled=True),
    )
    flipped = new_master.T
    col_payload, col_scale = quantize_blocks(flipped)
    stacked_payload, stacked_scale = (
        lax.all_gather(col_payload[None], "shard", axis=0, tiled=True),
        lax.all_gather(col_scale[None], "shard", axis=0, tiled=True),
    )
    col_copy, col_scales = (
        lax.all_to_all(stacked_payload, "tp", split_axis=1, concat_axis=2, tiled=True),
        lax.all_to_all(stacked_scale, "tp", split_axis=1, concat_axis=2, tiled=True),
    )
    return (new_master, new_first, new_second, row_copy, row_scales, col_copy, col_scales)


def solution(mesh):
    in_specs = (P("tp", "shard"), P("tp", "shard"), P("tp", "shard"), P("tp", "shard"), P())
    out_specs = (
        P("tp", "shard"),
        P("tp", "shard"),
        P("tp", "shard"),
        P("tp", None),
        P("tp", None),
        P(None, "tp", None),
        P(None, "tp", None),
    )
    return jax.shard_map(body, mesh=mesh, in_specs=in_specs, out_specs=out_specs, check_vma=False)
```

profile of v0, /device:TPU:1, one launch (start us, length us, event | category | flops | bytes accessed | tf_op | source)
XLA Modules:
  0.0 264.3 jit_solution(14375529181285294305)
XLA Ops:
  7.2 0.0 all-gather.7.cloned.1.call-start
  7.9 1.2 copy.35
  9.2 1.2 copy.37
  10.4 2.0 copy.38
  12.5 1.1 copy.36
  13.6 1.5 abs_bitcast_fusion
  15.0 0.2 copy.39
  15.2 0.1 bitcast_reduce_fusion
  15.4 0.2 copy.40
  15.6 0.8 fusion.2
  16.4 0.0 all-gather.7.cloned.1.call-update
  16.4 35.3 %all-gather.1 = bf16[4096,16]{0,1:T(8,128)(2,1)S(1)} all-gather(bf16[256,16]{0,1:T(8,128)(2,1)S(1)} %multiply_convert_fusion), channel_id=3, replica_groups=mesh['shard'=16,'tp'=16] {'shard'}, dimensions={0}, use_global_device_ids=true | all-gather | bytes 139264 | tf_op jit(solution)/shard_map/all_gather | solution.py:46
  51.7 0.9 copy.44
  52.6 1.8 reshape.63
  54.4 6.3 %all-to-all-start.1 = ((bf16[16,2,2048]{2,1,0:T(2,128)(2,1)}), bf16[16,2,2048]{2,1,0:T(2,128)(2,1)S(1)}, u32[]{:S(2)}, u32[]{:S(2)}) async-start(bf16[16,2,2048]{2,1,0:T(2,128)(2,1)} %reshape.63), calls=%async_computation.1 | async-start | bytes 262144 | tf_op jit(solution)/shard_map/all_to_all | solution.py:50
  60.7 0.0 all-gather.5.cloned.1.call-start
  60.8 0.1 bitcast_reduce_fusion.1
  60.8 0.8 fusion.3
  61.6 0.0 all-gather.5.cloned.1.call-update
  61.6 32.4 %all-gather.7.cloned.1.call-done = bf16[4096,512]{1,0:T(8,128)(2,1)} async-done(((bf16[256,512]{1,0:T(8,128)(2,1)}), bf16[4096,512]{1,0:T(8,128)(2,1)}) %all-gather.7.cloned.1.call-update) | async-done | bytes 4194320 | tf_op jit(solution)/shard_map/all_gather | solution.py:45
  94.0 6.5 %copy.41 = bf16[16,256,512]{2,0,1:T(8,128)(2,1)} copy(bf16[16,256,512]{2,1,0:T(8,128)(2,1)} %bitcast.36) | data formatting | bytes 8388608 | tf_op jit(solution)/shard_map/all_gather | solution.py:45
  100.6 0.0 all-to-all-done.1
  100.6 8.9 %all-to-all-start = ((bf16[16,256,512]{2,0,1:T(8,128)(2,1)}), bf16[16,256,512]{2,0,1:T(8,128)(2,1)}, u32[]{:S(2)}, u32[]{:S(2)}) async-start(bf16[16,256,512]{2,0,1:T(8,128)(2,1)} %copy.41), calls=%async_computation | async-start | bytes 8388608 | tf_op jit(solution)/shard_map/all_to_all | solution.py:49
  109.5 1.0 copy.47
  110.5 119.6 %all_gather.13 = bf16[512,128]{0,1:T(8,128)(2,1)S(1)} all-gather(bf16[512,8]{0,1:T(8,128)(2,1)S(1)} %get-tuple-element.33), channel_id=1, replica_groups=mesh['shard'=16,'tp'=16] {'shard'}, dimensions={1}, use_global_device_ids=true | all-gather | bytes 139264 | tf_op jit(solution)/shard_map/all_gather | solution.py:40
  230.1 0.8 copy.51
  230.9 1.0 copy.48
  231.9 1.0 copy.49
  232.9 0.7 reshape.64
  233.6 2.0 copy.46
  235.6 1.7 all_to_all.33
  237.2 0.0 all-gather.5.cloned.1.call-done
  237.2 6.3 %copy.50 = bf16[512,4096]{1,0:T(8,128)(2,1)} copy(bf16[512,4096]{0,1:T(8,128)(2,1)} %all-gather.5.cloned.1.call-done) | data formatting | bytes 8388608
  243.5 0.0 all-to-all-done
  243.5 6.5 %copy.43 = bf16[16,16,16,512]{3,2,1,0:T(8,128)(2,1)} copy(bf16[16,16,16,512]{3,0,1,2:T(8,128)(2,1)} %bitcast.11) | data formatting | bytes 8388608 | tf_op jit(solution)/shard_map/all_to_all | solution.py:49
  250.0 7.4 %all_to_all.29 = bf16[16,16,8192]{2,1,0:T(8,128)(2,1)} reshape(bf16[16,16,16,512]{3,2,1,0:T(8,128)(2,1)} %copy.43) | data formatting | bytes 8388608 | tf_op jit(solution)/shard_map/all_to_all | solution.py:49
  (4 shorter events, 0.1 us)
Async XLA Ops:
  7.2 86.9 %all-gather.7.cloned.1.call-start = ((), (), s32[]{:S(2)}) async-start(), calls=%async_computation.3 | async-start | bytes 4456448 | tf_op jit(solution)/shard_map/all_gather | solution.py:45
  54.4 46.2 %all-to-all-start.1 = ((bf16[16,2,2048]{2,1,0:T(2,128)(2,1)}), bf16[16,2,2048]{2,1,0:T(2,128)(2,1)S(1)}, u32[]{:S(2)}, u32[]{:S(2)}) async-start(bf16[16,2,2048]{2,1,0:T(2,128)(2,1)} %reshape.63), calls=%async_computation.1 | async-start | bytes 262144 | tf_op jit(solution)/shard_map/all_to_all | solution.py:50
  60.7 176.5 %all-gather.5.cloned.1.call-start = ((), (), s32[]{:S(2)}) async-start(), calls=%async_computation.2 | async-start | bytes 4456448 | tf_op jit(solution)/shard_map/all_gather | solution.py:39
  100.6 142.9 %all-to-all-start = ((bf16[16,256,512]{2,0,1:T(8,128)(2,1)}), bf16[16,256,512]{2,0,1:T(8,128)(2,1)}, u32[]{:S(2)}, u32[]{:S(2)}) async-start(bf16[16,256,512]{2,0,1:T(8,128)(2,1)} %copy.41), calls=%async_computation | async-start | bytes 8388608 | tf_op jit(solution)/shard_map/all_to_all | solution.py:49
Sparse Core Ops, SparseCore 0:
  16.5 77.4 all-gather.6
  97.3 102.2 all-gather.4
where the time goes:
time: 265 us; the launch traced here: 264 us
  blocking collectives  155 us (58%)
  local copies, waits for them, and re-layouts  43.5 us (16%)
  waiting for transfers between devices  32.4 us (12%)
  starting transfers between devices  15.3 us (6%)
  between operations  14.9 us (6%)
  other arithmetic  3.19 us (1%)
    all_gather x1, blocking collectives, body(): lax.all_gather(row_scale, 'shard', axis=1, tiled=True)  120 us
    all_gather x1, blocking collectives, body(): lax.all_gather(col_scale[None], 'shard', axis=0, tiled=True)  35.3 us
    all_gather x1, waiting for transfers between devices, body(): lax.all_gather(col_payload[None], 'shard', axis=0, tiled=True)  32.4 us
    unnamed x12, local copies, waits for them, and re-layouts  18.1 us
    all_to_all x2, local copies, waits for them, and re-layouts, body(): lax.all_to_all(stacked_payload, 'tp', split_axis=1, concat_axis=2, tiled=...  13.9 us
    all_to_all x1, starting transfers between devices, body(): lax.all_to_all(stacked_payload, 'tp', split_axis=1, concat_axis=2, tiled=...  8.92 us
    all_gather x1, local copies, waits for them, and re-layouts, body(): lax.all_gather(col_payload[None], 'shard', axis=0, tiled=True)  6.54 us
    all_to_all x1, starting transfers between devices, body(): lax.all_to_all(stacked_scale, 'tp', split_axis=1, concat_axis=2, tiled=True)  6.31 us
  transfers between devices with their start and end apart: 4, of which 1 were waited for; matrix products, arithmetic and copies ran while one was open for 9% of the time, Pallas kernels for 0%

commit v1 on v0

v1 whole, which is shorter than its diff:
```python
import jax
import jax.numpy as jnp
from jax import lax
from jax.experimental import pallas as pl
from jax.experimental.pallas import tpu as pltpu
from jax.sharding import PartitionSpec as P

beta_one = 0.9
beta_two = 0.95
learn_rate = 0.02
epsilon = 1e-08
floor_value = 0.008
scale_unit = 64.0
block_size = 32

MESH = pl.DeviceIdType.MESH
BF16 = jnp.bfloat16
F32 = jnp.float32

ROWS, COLS, CHUNKS = 512, 256, 4
STEP = ROWS // CHUNKS
VMEM_LIMIT = 24 * 2**20

ROW_SCALES, COL_SCALES, ITEMS = 16, 17, 18

STEPS = (
    (0,), (1,), (2,), (3,), (0, 1), (8,), (2, 3), (4,), (5,), (9,), (15,), (10,), (14,), (8, 5), (11,), (13,),
    (4, 9), (6,), (10, 15), (7,), (12,), (14, 11), (6, 13), (12, 7),
)
WINDOW, ARRIVAL = 2, 3
SMALL = {7: (16,), 13: (17,), 11: (16, None), 17: (None, 17)}
Z_NEAR = (1, 7, 2, 6)
Z_LATER = {7: ((1, 7), (3, 5), ()), 10: ((2, 6), (), (2, 3)), 13: ((3, 5), (4,), ())}
COLUMNS_AT, ROW_SCALES_AT = 5, 20


def place():
    shard, tp = lax.axis_index("shard"), lax.axis_index("tp")
    return shard // 4, (shard // 2) % 2, shard % 2, tp // 4, tp % 4


def device(x, zh, core, zl, y):
    return (x * 4 + zh * 2 + core, zl * 4 + y)


def gather_kernel(
    step_ref, master, first, second, grad,
    new_master, new_first, new_second, row_out, row_scale_out, col_out, cs_out,
    master_v, first_v, second_v, grad_v,
    row_s, col_s, padded, flipped, flipped_s, held, held_s, sums, gathered_s, rs,
    load_sem, send_sem, left_sem, right_sem, opp_sem, sib_sem,
    zrow_sem, zrs_sem, y_sem, ys_sem, z_sem, zs_sem, right_sent, left_sent, row_sent, z_sent,
):
    x, zh, core, zl, y = place()
    z = zh * 4 + zl

    def along(dx=0, dy=0, dz=0, dcore=0):
        zz = (z + dz) % 8
        return device((x + dx) % 4, zz // 4, (core + dcore) % 2, zz % 4, (y + dy) % 4)

    partners = [(0, 0, dz, 0) for dz in (4, 3, 5, 2, 6, 1, 7)]
    partners += [(1, 0, 0, 0), (3, 0, 0, 0), (0, 2, 0, 0), (0, 1, 0, 0), (0, 3, 0, 0), (0, 0, 0, 1)]
    barrier = pltpu.get_barrier_semaphore()
    for partner in partners:
        pl.semaphore_signal(barrier, inc=1, device_id=along(*partner), device_id_type=MESH)

    loads = []
    for i in range(CHUNKS):
        part = pl.ds(i * STEP, STEP)
        loads.append([
            pltpu.make_async_copy(src.at[part], dst.at[part], load_sem.at[i, j])
            for j, (src, dst) in enumerate(
                ((master, master_v), (first, first_v), (second, second_v), (grad, grad_v))
            )
        ])
        for copy in loads[-1]:
            copy.start()

    def row_window(i, xx, half, cc):
        return row_out.at[xx, half, cc, pl.ds(i * STEP, STEP)]

    def view(item, dx):
        xx = (x + dx) % 4
        if item < 4:
            return row_window(item, xx, zh, core)
        if item < 8:
            return row_window(item - 4, xx, 1 - zh, core)
        if item < 16:
            source = (z + 16 - item) % 8
            lanes = pl.multiple_of((source % 4) * 4 * ROWS, 4 * ROWS)
            return col_out.at[xx, source // 4, core, :, pl.ds(lanes, 4 * ROWS)]
        return (rs if item == ROW_SCALES else cs_out).at[xx, :, core]

    def kind(item):
        return 0 if item < 8 else 1 if item < 16 else item - 14

    def remote(src, dst, sent, received, target):
        pltpu.make_async_remote_copy(
            src_ref=src, dst_ref=dst, send_sem=sent, recv_sem=received,
            device_id=target, device_id_type=MESH,
        ).start()

    def arrived(ref, sem):
        pltpu.make_async_copy(ref, ref, sem).wait()

    def move(item, dx, received, target):
        ref = view(item, dx)
        remote(ref, ref, send_sem.at[kind(item)], received, target)

    def to_sibling(item, dx):
        move(item, dx, sib_sem.at[kind(item)], along(dcore=1))

    def row_across(i):
        ref = row_window(i, x, zh, core)
        remote(ref, ref, row_sent.at[i], zrow_sem.at[i], along(dz=4))

    def z_across(dz):
        there = (z + dz) % 8 % 4
        remote(held.at[there], view(8, 0), z_sent.at[dz], z_sem.at[dz], along(dz=dz))

    waited = set()

    def arrive(side, item):
        if (side, item) not in waited:
            waited.add((side, item))
            dx, sem = {"left": (3, left_sem), "right": (1, right_sem), "opposite": (2, opp_sem)}[side]
            arrived(view(item, dx), sem.at[item])
            to_sibling(item, dx)

    def arrivals(group):
        if len(group) == 1:
            arrive("left", group[0])
            arrive("right", group[0])
            return
        for item in group:
            if item is not None:
                arrive("opposite", item)

    def send(group, right_sent, left_sent):
        if len(group) == 1:
            item = group[0]
            at_hand(item)
            ref = view(item, 0)
            remote(ref, ref, right_sent, left_sem.at[item], along(dx=1))
            remote(ref, ref, left_sent, right_sem.at[item], along(dx=3))
            to_sibling(item, 0)
            return
        item, other = group
        if item is not None:
            arrive("left", item)
            remote(view(item, 3), view(item, 3), right_sent, opp_sem.at[item], along(dx=1))
        if other is not None:
            arrive("right", other)
            remote(view(other, 1), view(other, 1), left_sent, opp_sem.at[other], along(dx=3))

    def at_hand(item):
        if 4 <= item < 8:
            arrived(row_window(item - 4, x, 1 - zh, core), zrow_sem.at[item - 4])
        elif 8 <= item < 16:
            arrived(view(item, 0), z_sem.at[item - 8])
        elif item == ROW_SCALES:
            arrived(rs.at[x, 1 - zh, core], zrs_sem.at[0])
        elif item == COL_SCALES:
            arrived(gathered_s, zs_sem.at[0])
            for half in range(2):
                pairs = gathered_s[half].astype(F32)
                low, high = pairs[0] + pairs[1], pairs[2] + pairs[3]
                cs_out[x, half, core] = jnp.concatenate([low, high], axis=1).astype(BF16)

    def sent(step):
        if ("sent", step) not in waited:
            waited.add(("sent", step))
            for sems in (right_sent, left_sent):
                arrived(row_out.at[0, 0, 0, :STEP], sems.at[step % WINDOW])

    def step_out(step):
        if step >= WINDOW:
            sent(step - WINDOW)
        send(STEPS[step], right_sent.at[step % WINDOW], left_sent.at[step % WINDOW])

    steps_done = jnp.full((8, 128), step_ref[0].astype(F32), F32)
    corr_one = (1.0 - jnp.power(beta_one, steps_done))[0:1, 0:1]
    corr_two = (1.0 - jnp.power(beta_two, steps_done))[0:1, 0:1]

    def scale(blocks):
        largest = jnp.max(jnp.abs(blocks), axis=1)
        scales = (scale_unit * jnp.maximum(largest, floor_value)).astype(BF16).astype(F32)
        return scales, blocks * (scale_unit / scales)[:, None, :]

    for i in range(CHUNKS):
        part = pl.ds(i * STEP, STEP)
        for copy in loads[i]:
            copy.wait()
        g = grad_v[part, :].astype(F32)
        nf = beta_one * first_v[part, :] + (1.0 - beta_one) * g
        nv = beta_two * second_v[part, :] + (1.0 - beta_two) * g * g
        update = nf / corr_one / (jnp.sqrt(nv / corr_two) + epsilon)
        m = master_v[part, :] - learn_rate * update
        new_first[part, :] = nf
        new_second[part, :] = nv
        new_master[part, :] = m

        scales, scaled = scale(m.T.reshape(COLS // block_size, block_size, STEP))
        row_s[:, part] = scales
        row_out[x, zh, core, part, :] = scaled.reshape(COLS, STEP).T.astype(BF16)
        if i == 0:
            pl.semaphore_wait(barrier, len(partners))
        if i < WINDOW:
            step_out(i)
            row_across(i)

        scales, scaled = scale(m.reshape(STEP // block_size, block_size, COLS))
        col_s[4 * i : 4 * i + 4, :] = scales
        flipped[:, part] = scaled.reshape(STEP, COLS).T.astype(BF16)

    values = flipped.reshape(4, 4, 16, ROWS)
    lanes = pl.ds(pl.multiple_of(y * ROWS, ROWS), ROWS)
    for dy in (2, 1, 3):
        there = (y + dy) % 4
        remote(values.at[:, there], held.at[:, :, lanes], send_sem.at[6], y_sem.at[0], along(dy=dy))
    pltpu.make_async_copy(values.at[:, y], held.at[:, :, lanes], y_sem.at[0]).start()

    own = row_s[...]
    rs[x, zh, core] = jnp.concatenate([own[:, :COLS], own[:, COLS:]], axis=0).astype(BF16)
    ref = rs.at[x, zh, core]
    remote(ref, ref, send_sem.at[5], zrs_sem.at[0], along(dz=4))

    padded[...] = jnp.zeros_like(padded)
    padded[pl.ds(pl.multiple_of(((zl * 4 + y) % 8) * 16, 16), 16), :] = col_s[...]
    flipped_s[...] = padded[...].T.astype(BF16)
    value_scales = flipped_s.reshape(4, 4, 16, 128)
    for dy in (2, 1, 3):
        there = (y + dy) % 4
        remote(value_scales.at[:, there], held_s.at[y], send_sem.at[7], ys_sem.at[0], along(dy=dy))
    pltpu.make_async_copy(value_scales.at[:, y], held_s.at[y], ys_sem.at[0]).start()

    for step in range(WINDOW, len(STEPS)):
        if step == COLUMNS_AT:
            arrived(held, y_sem.at[0])
            for i in range(WINDOW):
                arrived(row_window(i, x, zh, core), row_sent.at[i])
            for dz in Z_NEAR:
                z_across(dz)
            pltpu.make_async_copy(held.at[zl], view(8, 0), z_sem.at[0]).start()
        step_out(step)
        if step == COLUMNS_AT:
            arrived(held_s, ys_sem.at[0])
            parts = held_s[...].astype(F32)
            sums[...] = (parts[0] + parts[1] + parts[2] + parts[3]).astype(BF16)
            pltpu.make_async_copy(sums.at[zl], gathered_s.at[zh, zl], zs_sem.at[0]).start()
            for dz in range(1, 8):
                there = (z + dz) % 8 % 4
                remote(sums.at[there], gathered_s.at[zh, zl], send_sem.at[9], zs_sem.at[0], along(dz=dz))
        if step in Z_LATER:
            done, columns, rows = Z_LATER[step]
            for dz in done:
                arrived(view(8, 0), z_sent.at[dz])
            for dz in columns:
                z_across(dz)
            for i in rows:
                row_across(i)
        if step in SMALL:
            group = SMALL[step]
            sems = send_sem.at[max(i or 0 for i in group) - 14]
            send(group, sems, sems)
        if step >= ARRIVAL:
            arrivals(STEPS[step - ARRIVAL])
        if step - ARRIVAL in SMALL:
            arrivals(SMALL[step - ARRIVAL])
        if step == ROW_SCALES_AT + 1:
            arrived(rs.at[:, :, 0], sib_sem.at[2])
            scales = rs[...].astype(F32).reshape(16, 16, COLS)
            for half in range(2):
                one = scales[:, 8 * half : 8 * half + 8].reshape(128, COLS)
                row_scale_out[COLS * half : COLS * (half + 1), :] = one.T.astype(BF16)
    for step in range(len(STEPS) - ARRIVAL, len(STEPS)):
        arrivals(STEPS[step])

    arrived(cs_out.at[:, :, 0], sib_sem.at[3])
    arrived(row_out.at[:, :, 0], sib_sem.at[0])
    arrived(col_out.at[:, :, 0], sib_sem.at[1])
    arrived(flipped.at[: 3 * 64], send_sem.at[6])
    arrived(flipped_s.at[: 3 * 64], send_sem.at[7])
    arrived(rs.at[0, 0, 0], send_sem.at[5])
    arrived(row_out.at[0, 0, 0, :112, :128], send_sem.at[9])
    arrived(row_out.at[:, :, 0], send_sem.at[0])
    arrived(col_out.at[:, :, 0], send_sem.at[1])
    arrived(row_out.at[0, 0, 0, :224], send_sem.at[2])
    arrived(row_out.at[0, 0, 0, :224], send_sem.at[3])
    for i in range(WINDOW, CHUNKS):
        arrived(row_window(i, x, zh, core), row_sent.at[i])
    arrived(view(8, 0), z_sent.at[4])
    for step in range(len(STEPS)):
        sent(step)


def write_kernel(*refs):
    half = len(refs) // 2
    sems = refs[-1]
    pairs = []
    for src, dst in zip(refs[:half], refs[half : 2 * half]):
        if src.shape == dst.shape:
            pairs.append((src, dst))
            continue
        for s in range(16):
            pairs.append((src.at[s // 4, s // 2 % 2, s % 2], dst.at[:, pl.ds(s * COLS, COLS)]))
    copies = [pltpu.make_async_copy(src, dst, sems.at[i]) for i, (src, dst) in enumerate(pairs)]
    for copy in copies:
        copy.start()
    for copy in copies:
        copy.wait()


def body(master, first_moment, second_moment, gradient, step_count):
    block = (ROWS, COLS)
    shapes = [
        (block, F32), (block, F32), (block, F32),
        ((ROWS, 16 * COLS), BF16), ((ROWS, 128), BF16),
        ((4, 2, 2, 16, 16 * ROWS), BF16), ((4, 2, 2, 16, 256), BF16),
    ]
    held_shapes = shapes[:3] + [((4, 2, 2, ROWS, COLS), BF16)] + shapes[4:]
    vmem = pl.BlockSpec(memory_space=pltpu.VMEM)
    hbm = pl.BlockSpec(memory_space=pltpu.HBM)
    dma = pltpu.SemaphoreType.DMA
    place_in = pltpu.with_memory_space_constraint
    held = pl.pallas_call(
        gather_kernel,
        name="gather_copies",
        out_shape=[pltpu.VMEM(shape, dtype) for shape, dtype in held_shapes],
        in_specs=[pl.BlockSpec(memory_space=pltpu.SMEM)] + [hbm] * 4,
        out_specs=[vmem] * 7,
        scratch_shapes=[
            pltpu.VMEM(block, F32), pltpu.VMEM(block, F32), pltpu.VMEM(block, F32), pltpu.VMEM(block, BF16),
            pltpu.VMEM((8, ROWS), F32), pltpu.VMEM((16, COLS), F32), pltpu.VMEM((128, COLS), F32),
            pltpu.VMEM((COLS, ROWS), BF16), pltpu.VMEM((COLS, 128), BF16),
            pltpu.VMEM((4, 16, 4 * ROWS), BF16), pltpu.VMEM((4, 4, 16, 128), BF16),
            pltpu.VMEM((4, 16, 128), BF16), pltpu.VMEM((2, 4, 16, 128), BF16),
            pltpu.VMEM((4, 2, 2, 16, 256), BF16),
            dma((CHUNKS, 4)), dma((10,)), dma((ITEMS,)), dma((ITEMS,)), dma((ITEMS,)), dma((4,)),
            dma((4,)), dma((1,)), dma((1,)), dma((1,)), dma((8,)), dma((1,)),
            dma((WINDOW,)), dma((WINDOW,)), dma((CHUNKS,)), dma((8,)),
        ],
        compiler_params=pltpu.CompilerParams(
            collective_id=0, has_side_effects=True, vmem_limit_bytes=VMEM_LIMIT
        ),
    )(step_count, *(place_in(a, pltpu.HBM) for a in (master, first_moment, second_moment, gradient)))
    new_master, new_first, new_second, row_copy, row_scales, col_copy, col_scales = pl.pallas_call(
        write_kernel,
        name="write_results",
        out_shape=[jax.ShapeDtypeStruct(shape, dtype) for shape, dtype in shapes],
        in_specs=[vmem] * 7,
        out_specs=[hbm] * 7,
        scratch_shapes=[dma((22,))],
        compiler_params=pltpu.CompilerParams(vmem_limit_bytes=VMEM_LIMIT),
    )(*(place_in(a, pltpu.VMEM) for a in held))
    return (
        new_master, new_first, new_second, row_copy, row_scales,
        col_copy.reshape(16, 16, 16 * ROWS), col_scales.reshape(16, 16, 256),
    )


def solution(mesh):
    blocks = P("tp", "shard")
    in_specs = (blocks, blocks, blocks, blocks, P())
    out_specs = (
        blocks, blocks, blocks, P("tp", None), P("tp", None), P(None, "tp", None), P(None, "tp", None),
    )
    return jax.shard_map(body, mesh=mesh, in_specs=in_specs, out_specs=out_specs, check_vma=False)
```

time: 265 us -> 54.7 us (0.21)
  blocking collectives: 155 us -> 0 us
  Pallas kernels: 0 us -> 53.3 us
  local copies, waits for them, and re-layouts: 43.5 us -> 0 us
  waiting for transfers between devices: 32.4 us -> 0 us
  starting transfers between devices: 15.3 us -> 0 us
  between operations: 14.9 us -> 1.29 us
  other arithmetic: 3.19 us -> 0 us
    all_gather x2 -> x0, blocking collectives: 155 us -> none  [the longest x1 120 us: body(): lax.all_gather(row_scale, 'shard', axis=1, tiled=True)]
    pallas_call x0 -> x2, Pallas kernels: none -> 53.3 us  [the longest x1 49.2 us: body(): pl.pallas_call(gather_kernel, name='gather_copies', out_shape=[pltpu.VMEM...]
    all_gather x2 -> x0, waiting for transfers between devices: 32.4 us -> none  [the longest x1 32.4 us: body(): lax.all_gather(col_payload[None], 'shard', axis=0, tiled=True)]
    unnamed x12 -> x0, local copies, waits for them, and re-layouts: 18.1 us -> none
    all_to_all x4 -> x0, local copies, waits for them, and re-layouts: 17.5 us -> none  [the longest x2 13.9 us: body(): lax.all_to_all(stacked_payload, 'tp', split_axis=1, concat_axis=2, tiled=...]
    all_to_all x2 -> x0, starting transfers between devices: 15.2 us -> none  [the longest x1 8.92 us: body(): lax.all_to_all(stacked_payload, 'tp', split_axis=1, concat_axis=2, tiled=...]
    all_gather x2 -> x0, local copies, waits for them, and re-layouts: 7.49 us -> none  [the longest x1 6.54 us: body(): lax.all_gather(col_payload[None], 'shard', axis=0, tiled=True)]
  transfers between devices with their start and end apart: 4 -> 0, of which waited for: 1 -> 0; matrix products, arithmetic and copies ran while one was open for 9% -> 0% of each run, Pallas kernels for 0% -> 0%
where the time goes in v1:
time: 54.7 us; the launch traced here: 54.6 us
  Pallas kernels  53.3 us (97%)
  between operations  1.29 us (2%)
    pallas_call x1, Pallas kernels, body(): pl.pallas_call(gather_kernel, name='gather_copies', out_shape=[pltpu.VMEM...  49.2 us
    pallas_call x1, Pallas kernels, body(): pl.pallas_call(write_kernel, name='write_results', out_shape=[jax.ShapeDt...  4.1 us

profile of v1, /device:TPU:1, one launch (start us, length us, event | category | flops | bytes accessed | tf_op | source)
XLA Modules:
  0.0 54.6 jit_solution(1810733242119752137)
XLA Ops:
  1.3 49.2 %gather_copies.1 = (f32[512,256]{1,0:T(8,128)S(1)}, f32[512,256]{1,0:T(8,128)S(1)}, f32[512,256]{1,0:T(8,128)S(1)}, bf16[4,2,2,512,256]{4,3,2,1,0:T(8,128)(2,1)S...) custom-call(s32[1]{0:T(128)S(6)} %copy.12.step_ref, ...), custom_call_target="tpu_custom_call" | custom-call | tf_op jit(solution)/shard_map/gather_copies/pallas_call | solution.py:326
  50.5 4.1 %write_results.1 = (f32[512,256]{1,0:T(8,128)}, f32[512,256]{1,0:T(8,128)}, f32[512,256]{1,0:T(8,128)}, bf16[512,4096]{1,0:T(8,128)(2,1)}, bf16[512,128]{1,0:T(8...) custom-call(f32[512,256]{1,0:T(8,128)S(1)} %get-tuple-element.21.refs_0_, ...), custom_call_target="tpu_custom_call" | custom-call | tf_op jit(solution)/shard_map/write_results/pallas_call | solution.py:347

commit v2 on v1

--- a/solution.py
+++ b/solution.py
@@ -25,12 +25,12 @@
 
 STEPS = (
     (0,), (1,), (2,), (3,), (0, 1), (8,), (2, 3), (4,), (5,), (9,), (15,), (10,), (14,), (8, 5), (11,), (13,),
-    (4, 9), (6,), (10, 15), (7,), (12,), (14, 11), (6, 13), (12, 7),
+    (4, 9), (12,), (10, 15), (6,), (7,), (14, 11), (12, 13), (6, 7),
 )
-WINDOW, ARRIVAL = 2, 3
+WINDOW, ARRIVAL = 3, 4
 SMALL = {7: (16,), 13: (17,), 11: (16, None), 17: (None, 17)}
 Z_NEAR = (1, 7, 2, 6)
-Z_LATER = {7: ((1, 7), (3, 5), ()), 10: ((2, 6), (), (2, 3)), 13: ((3, 5), (4,), ())}
+Z_LATER = {6: ((1, 7), (3, 5), ()), 9: ((2, 6), (4,), ()), 12: ((3, 5), (), (2, 3))}
 COLUMNS_AT, ROW_SCALES_AT = 5, 20
 
 
@@ -187,6 +187,16 @@
         scales = (scale_unit * jnp.maximum(largest, floor_value)).astype(BF16).astype(F32)
         return scales, blocks * (scale_unit / scales)[:, None, :]
 
+    values = flipped.reshape(4, 4, 16, ROWS)
+
+    def y_across(half):
+        here = pl.ds(half * COLS, COLS)
+        lanes = pl.ds(pl.multiple_of(y * ROWS + half * COLS, COLS), COLS)
+        for dy in (2, 1, 3):
+            there = (y + dy) % 4
+            remote(values.at[:, there, :, here], held.at[:, :, lanes], send_sem.at[6], y_sem.at[0], along(dy=dy))
+        pltpu.make_async_copy(values.at[:, y, :, here], held.at[:, :, lanes], y_sem.at[0]).start()
+
     for i in range(CHUNKS):
         part = pl.ds(i * STEP, STEP)
         for copy in loads[i]:
@@ -207,18 +217,14 @@
             pl.semaphore_wait(barrier, len(partners))
         if i < WINDOW:
             step_out(i)
+        if i < 2:
             row_across(i)
 
         scales, scaled = scale(m.reshape(STEP // block_size, block_size, COLS))
         col_s[4 * i : 4 * i + 4, :] = scales
         flipped[:, part] = scaled.reshape(STEP, COLS).T.astype(BF16)
-
-    values = flipped.reshape(4, 4, 16, ROWS)
-    lanes = pl.ds(pl.multiple_of(y * ROWS, ROWS), ROWS)
-    for dy in (2, 1, 3):
-        there = (y + dy) % 4
-        remote(values.at[:, there], held.at[:, :, lanes], send_sem.at[6], y_sem.at[0], along(dy=dy))
-    pltpu.make_async_copy(values.at[:, y], held.at[:, :, lanes], y_sem.at[0]).start()
+        if i % 2 == 1:
+            y_across(i // 2)
 
     own = row_s[...]
     rs[x, zh, core] = jnp.concatenate([own[:, :COLS], own[:, COLS:]], axis=0).astype(BF16)
@@ -237,8 +243,6 @@
     for step in range(WINDOW, len(STEPS)):
         if step == COLUMNS_AT:
             arrived(held, y_sem.at[0])
-            for i in range(WINDOW):
-                arrived(row_window(i, x, zh, core), row_sent.at[i])
             for dz in Z_NEAR:
                 z_across(dz)
             pltpu.make_async_copy(held.at[zl], view(8, 0), z_sem.at[0]).start()
@@ -287,7 +291,7 @@
     arrived(col_out.at[:, :, 0], send_sem.at[1])
     arrived(row_out.at[0, 0, 0, :224], send_sem.at[2])
     arrived(row_out.at[0, 0, 0, :224], send_sem.at[3])
-    for i in range(WINDOW, CHUNKS):
+    for i in range(0, CHUNKS):
         arrived(row_window(i, x, zh, core), row_sent.at[i])
     arrived(view(8, 0), z_sent.at[4])
     for step in range(len(STEPS)):

time: 54.7 us -> 54.2 us (level)
  no operation moved by 1% of the time
where the time goes in v2:
time: 54.2 us; the launch traced here: 54.1 us
  Pallas kernels  52.8 us (97%)
  between operations  1.29 us (2%)
    pallas_call x1, Pallas kernels, body(): pl.pallas_call(gather_kernel, name='gather_copies', out_shape=[pltpu.VMEM...  48.7 us
    pallas_call x1, Pallas kernels, body(): pl.pallas_call(write_kernel, name='write_results', out_shape=[jax.ShapeDt...  4.1 us

profile of v2, /device:TPU:1, one launch (start us, length us, event | category | flops | bytes accessed | tf_op | source)
XLA Modules:
  0.0 54.1 jit_solution(13524048562104600237)
XLA Ops:
  1.3 48.7 %gather_copies.1 = (f32[512,256]{1,0:T(8,128)S(1)}, f32[512,256]{1,0:T(8,128)S(1)}, f32[512,256]{1,0:T(8,128)S(1)}, bf16[4,2,2,512,256]{4,3,2,1,0:T(8,128)(2,1)S...) custom-call(s32[1]{0:T(128)S(6)} %copy.12.step_ref, ...), custom_call_target="tpu_custom_call" | custom-call | tf_op jit(solution)/shard_map/gather_copies/pallas_call | solution.py:330
  50.0 4.1 %write_results.1 = (f32[512,256]{1,0:T(8,128)}, f32[512,256]{1,0:T(8,128)}, f32[512,256]{1,0:T(8,128)}, bf16[512,4096]{1,0:T(8,128)(2,1)}, bf16[512,128]{1,0:T(8...) custom-call(f32[512,256]{1,0:T(8,128)S(1)} %get-tuple-element.21.refs_0_, ...), custom_call_target="tpu_custom_call" | custom-call | tf_op jit(solution)/shard_map/write_results/pallas_call | solution.py:351

commit v3 on v2

--- a/solution.py
+++ b/solution.py
@@ -280,9 +280,6 @@
     for step in range(len(STEPS) - ARRIVAL, len(STEPS)):
         arrivals(STEPS[step])
 
-    arrived(cs_out.at[:, :, 0], sib_sem.at[3])
-    arrived(row_out.at[:, :, 0], sib_sem.at[0])
-    arrived(col_out.at[:, :, 0], sib_sem.at[1])
     arrived(flipped.at[: 3 * 64], send_sem.at[6])
     arrived(flipped_s.at[: 3 * 64], send_sem.at[7])
     arrived(rs.at[0, 0, 0], send_sem.at[5])
@@ -296,6 +293,9 @@
     arrived(view(8, 0), z_sent.at[4])
     for step in range(len(STEPS)):
         sent(step)
+    arrived(cs_out.at[:, :, 0], sib_sem.at[3])
+    arrived(row_out.at[:, :, 0], sib_sem.at[0])
+    arrived(col_out.at[:, :, 0], sib_sem.at[1])
 
 
 def write_kernel(*refs):

time: 54.2 us -> 54.2 us (level)
  no operation moved by 1% of the time
where the time goes in v3:
time: 54.2 us; the launch traced here: 54.1 us
  Pallas kernels  52.8 us (97%)
  between operations  1.29 us (2%)
    pallas_call x1, Pallas kernels, body(): pl.pallas_call(gather_kernel, name='gather_copies', out_shape=[pltpu.VMEM...  48.7 us
    pallas_call x1, Pallas kernels, body(): pl.pallas_call(write_kernel, name='write_results', out_shape=[jax.ShapeDt...  4.1 us

profile of v3, /device:TPU:1, one launch (start us, length us, event | category | flops | bytes accessed | tf_op | source)
XLA Modules:
  0.0 54.1 jit_solution(5704032498697706295)
XLA Ops:
  1.3 48.7 %gather_copies.1 = (f32[512,256]{1,0:T(8,128)S(1)}, f32[512,256]{1,0:T(8,128)S(1)}, f32[512,256]{1,0:T(8,128)S(1)}, bf16[4,2,2,512,256]{4,3,2,1,0:T(8,128)(2,1)S...) custom-call(s32[1]{0:T(128)S(6)} %copy.12.step_ref, ...), custom_call_target="tpu_custom_call" | custom-call | tf_op jit(solution)/shard_map/gather_copies/pallas_call | solution.py:330
  50.0 4.1 %write_results.1 = (f32[512,256]{1,0:T(8,128)}, f32[512,256]{1,0:T(8,128)}, f32[512,256]{1,0:T(8,128)}, bf16[512,4096]{1,0:T(8,128)(2,1)}, bf16[512,128]{1,0:T(8...) custom-call(f32[512,256]{1,0:T(8,128)S(1)} %get-tuple-element.21.refs_0_, ...), custom_call_target="tpu_custom_call" | custom-call | tf_op jit(solution)/shard_map/write_results/pallas_call | solution.py:351
